TPU v7x, 512 devices: a whole 4x4x16 slice. The times are simulated.
512 devices in a mesh: dp: 64 (over y_hi, z, core), tensor: 8 (over x, y_lo).
Axes of the slice: x: 4, y: 4 (y_hi: 2, y_lo: 2; y = y_hi * 2 + y_lo), z: 16, core: 2. Of those that a mesh axis runs over, the one named last changes fastest.
Arguments:
- hidden: bfloat16 [16384, 8192], P('dp', 'tensor'), may hold values from -600 to 600, as said below
- norm_gain: bfloat16 [8192], replicated, may hold values from 0.099609375 to 1.8984375
- query_weight: bfloat16 [8192, 4096], P(('dp', 'tensor')), may hold values from -0.0625 to 0.0625
- key_weight: bfloat16 [8192, 1024], P(('dp', 'tensor')), may hold values from -0.0625 to 0.0625
- value_weight: bfloat16 [8192, 1024], P(('dp', 'tensor')), may hold values from -0.0625 to 0.0625
- query_bias: bfloat16 [4096], P('tensor'), may hold values from -2 to 8, as said below
- key_bias: bfloat16 [1024], P('tensor'), may hold values from -2 to 6, as said below
- value_bias: bfloat16 [1024], P('tensor'), may hold values from -3 to 3
- lengths: int32 [64, 4], P('dp'), may hold values from 1 to 128, 256 in all within a row
- page_table: int32 [64, 16], P('dp'), may hold values from 0 to 15, each once within a row
Outputs:
- attention: bfloat16 [16384, 4096], P('dp', 'tensor')
- cache_pages: bfloat16 [1024, 32, 2048], P('dp', None, 'tensor')
Inputs may be any that keep to these rules, and one draw needn't show every extreme that they name: `hidden`: the custom draw of the layer input. `query_bias`: the custom draw of the query bias. `key_bias`: the custom draw of the key bias. Each replica's lengths sum to 256, and its longest rollout has exactly 128 tokens. `page_table`: each replica's row is a permutation of its 16 pages.
All inputs are finite; a program needn't handle non-finite values.
Results may differ from a plain program's by a relative error of at most 0.0088.
Values may be sent and summed in bfloat16 or wider, within the bound.
A program may use at most 64 MiB of HBM per device.

v0:
```python
import jax
import jax.numpy as jnp
from jax import lax
from jax.sharding import PartitionSpec as P

HD = 128
ROLLS = 4
PAGE = 32
BLOCKS = 4
PAGES_REP = 16
rope_base = 1000000.0


def rotary(values_f, positions):
    halfway = HD // 2
    frequency = rope_base ** (-(jnp.arange(halfway, dtype=jnp.float32) * 2.0 / HD))
    angles = positions.astype(jnp.float32)[:, None] * frequency[None, :]
    cosine = jnp.cos(angles)[:, None, :]
    sine_part = jnp.sin(angles)[:, None, :]
    lower_half = values_f[..., :halfway]
    upper_half = values_f[..., halfway:]
    return jnp.concatenate(
        [
            lower_half * cosine - upper_half * sine_part,
            upper_half * cosine + lower_half * sine_part,
        ],
        axis=-1,
    )


def segments_of(length_row, token_count):
    ends = jnp.cumsum(length_row)
    starts = ends - length_row
    tok_index = jnp.arange(token_count, dtype=jnp.int32)
    segment = jnp.sum((tok_index[None, :] >= ends[:, None]).astype(jnp.int32), axis=0)
    onehot = segment[:, None] == jnp.arange(ROLLS, dtype=jnp.int32)[None, :]
    leading = jnp.sum(jnp.where(onehot, starts[None, :], 0), axis=1)
    return (segment, tok_index - leading, starts)


def attention_of(queries, key_rows, value_rows, segment):
    token_count = queries.shape[0]
    kv_heads = key_rows.shape[1]
    group_size = queries.shape[1] // kv_heads
    grouped = queries.reshape(token_count, kv_heads, group_size, HD)
    scores = jnp.einsum(
        "ikgd,jkd->kgij", grouped, key_rows, preferred_element_type=jnp.float32
    ) * HD ** (-0.5)
    tok_index = jnp.arange(token_count, dtype=jnp.int32)
    allowed = (segment[:, None] == segment[None, :]) & (tok_index[None, :] <= tok_index[:, None])
    scores = jnp.where(allowed[None, None], scores, -1e30)
    row_max = jnp.max(scores, axis=-1, keepdims=True)
    weights = jnp.exp(scores - row_max)
    weights = (weights / jnp.sum(weights, axis=-1, keepdims=True)).astype(jnp.bfloat16)
    mixed = jnp.einsum("kgij,jkd->ikgd", weights, value_rows, preferred_element_type=jnp.float32)
    return mixed.reshape(token_count, kv_heads * group_size * HD).astype(jnp.bfloat16)


def pages_of(kv_rows, length_row, starts, page_row):
    slots = jnp.arange(PAGES_REP, dtype=jnp.int32)
    owner = slots // BLOCKS
    within = slots % BLOCKS
    offsets = within[:, None] * PAGE + jnp.arange(PAGE, dtype=jnp.int32)[None, :]
    onehot = owner[:, None] == jnp.arange(ROLLS, dtype=jnp.int32)[None, :]
    owner_len = jnp.sum(jnp.where(onehot, length_row[None, :], 0), axis=1)
    owner_start = jnp.sum(jnp.where(onehot, starts[None, :], 0), axis=1)
    valid_slot = offsets < owner_len[:, None]
    source = jnp.where(valid_slot, owner_start[:, None] + offsets, 0)
    blocks_out = jnp.where(valid_slot[..., None], kv_rows[source], jnp.zeros((), jnp.bfloat16))
    empty = jnp.zeros((PAGES_REP, PAGE, kv_rows.shape[1]), jnp.bfloat16)
    return empty.at[page_row].set(blocks_out)


def column_slice(whole, parts_count, rank_index):
    width = whole.shape[1] // parts_count
    return lax.dynamic_slice_in_dim(whole, rank_index * width, width, 1)


def on_device(
    hidden,
    norm_gain,
    query_weight,
    key_weight,
    value_weight,
    query_bias,
    key_bias,
    value_bias,
    lengths,
    page_table,
):
    tokens = lax.all_gather(hidden, "tensor", axis=1, tiled=True)
    token_count = tokens.shape[0]
    tokens_f = tokens.astype(jnp.float32)
    meansq = jnp.mean(tokens_f * tokens_f, axis=-1, keepdims=True)
    normed = (tokens_f * lax.rsqrt(meansq + 1e-06) * norm_gain.astype(jnp.float32)).astype(
        jnp.bfloat16
    )
    length_row = lengths[0]
    segment, position, starts = segments_of(length_row, token_count)
    whole_query, whole_key, whole_value = (
        lax.all_gather(query_weight, "tensor", axis=0, tiled=True),
        lax.all_gather(key_weight, "tensor", axis=0, tiled=True),
        lax.all_gather(value_weight, "tensor", axis=0, tiled=True),
    )
    group_count = lax.axis_size("tensor")
    rank_index = lax.axis_index("tensor")
    local_query = column_slice(whole_query, group_count, rank_index)
    local_key = column_slice(whole_key, group_count, rank_index)
    local_value = column_slice(whole_value, group_count, rank_index)

    def add_rows(shard_rows):
        return jnp.dot(normed, shard_rows, preferred_element_type=jnp.float32)

    shard_rows = (
        lax.all_gather(local_query, "dp", axis=0, tiled=True),
        lax.all_gather(local_key, "dp", axis=0, tiled=True),
        lax.all_gather(local_value, "dp", axis=0, tiled=True),
    )
    proj_query = add_rows(shard_rows[0])
    proj_key = add_rows(shard_rows[1])
    proj_value = add_rows(shard_rows[2])
    kv_heads = proj_key.shape[1] // HD
    q_heads = proj_query.shape[1] // HD
    key_rows = rotary(
        (proj_key + key_bias.astype(jnp.float32)).reshape(token_count, kv_heads, HD), position
    ).astype(jnp.bfloat16)
    value_rows = (
        (proj_value + value_bias.astype(jnp.float32))
        .astype(jnp.bfloat16)
        .reshape(token_count, kv_heads, HD)
    )
    kv_rows = jnp.stack([key_rows, value_rows], axis=2).reshape(token_count, kv_heads * 2 * HD)
    cache_pages = pages_of(kv_rows, length_row, starts, page_table[0])
    queries = rotary(
        (proj_query + query_bias.astype(jnp.float32)).reshape(token_count, q_heads, HD), position
    ).astype(jnp.bfloat16)
    attention = attention_of(queries, key_rows, value_rows, segment)
    return (attention, cache_pages)


def solution(mesh):
    placed = (
        P("dp", "tensor"),
        P(),
        P(("dp", "tensor"), None),
        P(("dp", "tensor"), None),
        P(("dp", "tensor"), None),
        P("tensor"),
        P("tensor"),
        P("tensor"),
        P("dp", None),
        P("dp", None),
    )
    return jax.shard_map(
        on_device,
        mesh=mesh,
        in_specs=placed,
        out_specs=(P("dp", "tensor"), P("dp", None, "tensor")),
        check_vma=False,
    )
```

profile of v0, /device:TPU:1, one launch (start us, length us, event | category | flops | bytes accessed | tf_op | source)
XLA Modules:
  0.0 634.6 jit_solution(7657329097963163493)
XLA Ops:
  7.2 0.7 all-gather.12.cloned.1.call-update
  7.9 0.7 all-gather.6.cloned.1.call-update
  8.7 23.3 %all_gather.24 = bf16[128,1024]{1,0:T(8,128)(2,1)S(1)} all-gather(bf16[16,1024]{1,0:T(8,128)(2,1)} %param.13), channel_id=1, replica_groups=mesh['dp'=64,'tensor'=8] {'tensor'}, dimensions={0}, use_global_device_ids=true | all-gather | bytes 294912 | tf_op jit(solution)/shard_map/all_gather | solution.py:102
  32.7 24.8 %all_gather.22 = bf16[128,1024]{1,0:T(8,128)(2,1)S(1)} all-gather(bf16[16,1024]{1,0:T(8,128)(2,1)} %param.14), channel_id=1, replica_groups=mesh['dp'=64,'tensor'=8] {'tensor'}, dimensions={0}, use_global_device_ids=true | all-gather | bytes 294912 | tf_op jit(solution)/shard_map/all_gather | solution.py:103
  58.2 1.9 all-gather.12.cloned.1.call-done
  60.1 1.6 constant_dynamic-slice_fusion
  61.7 0.7 convert_element_type.62
  62.4 0.7 convert_element_type.69
  63.1 0.8 broadcast_in_dim.62
  63.9 0.7 convert_element_type.67
  65.2 0.7 fusion.27
  65.9 0.7 select_reduce_fusion.2
  67.0 0.7 fusion.26
  68.4 94.6 %all-gather.6.cloned.1.call-done = bf16[256,8192]{1,0:T(8,128)(2,1)} async-done(((bf16[256,1024]{1,0:T(8,128)(2,1)}), bf16[256,8192]{1,0:T(8,128)(2,1)}) %all-gather.6.cloned.1.call-update) | async-done | bytes 4194320 | tf_op jit(solution)/shard_map/all_gather | solution.py:91
  163.0 3.1 fusion
  166.1 147.7 %all-gather.10.cloned.1.call-done = bf16[8192,128]{1,0:T(8,128)(2,1)} async-done(((bf16[128,128]{1,0:T(8,128)(2,1)}), bf16[8192,128]{1,0:T(8,128)(2,1)}) %all-gather.10.cloned.1.call-update) | async-done | bytes 2097168 | tf_op jit(solution)/shard_map/all_gather | solution.py:116
  313.8 4.6 fusion.5
  318.7 136.4 %all-gather.8.cloned.1.call-done = bf16[8192,128]{1,0:T(8,128)(2,1)} async-done(((bf16[128,128]{1,0:T(8,128)(2,1)}), bf16[8192,128]{1,0:T(8,128)(2,1)}) %all-gather.8.cloned.1.call-update) | async-done | bytes 2097168 | tf_op jit(solution)/shard_map/all_gather | solution.py:117
  455.2 4.6 fusion.6
  459.9 2.0 gather_fusion
  462.0 1.0 scatter_fusion
  463.1 155.4 %all-gather.14.cloned.1.call-done = bf16[8192,512]{1,0:T(8,128)(2,1)} async-done(((bf16[128,512]{1,0:T(8,128)(2,1)}), bf16[8192,512]{1,0:T(8,128)(2,1)}) %all-gather.14.cloned.1.call-update) | async-done | bytes 8388624 | tf_op jit(solution)/shard_map/all_gather | solution.py:115
  618.5 7.0 %convolution_add_fusion = f32[256,512]{1,0:T(8,128)S(1)} fusion(bf16[8192,512]{1,0:T(8,128)(2,1)} %all-gather.14.cloned.1.call-done, f32[512]{0:T(512)S(1)} %convert_element_type.69, bf16[256,8192]{1,0:T(8,128)(2,1)} %all-gather.6.cloned.1.call-done, f32[8192]{0:T(1024)S(1)} %convert_element_type.62, f32[256]{0:T(256)S(1)} %add_rsqrt_fusion), kind=kOutput, calls=%fused_computation.10 | convolution fusion | flops 2156003328 | bytes 13143040 | tf_op jit(solution)/shard_map/dot_general | solution.py:112
  627.2 0.8 copy.29
  (36 shorter events, 5.4 us)
Async XLA Ops:
  7.2 52.9 %all-gather.12.cloned.1.call-start = ((), (), s32[]{:S(2)}) async-start(), calls=%async_computation.3 | async-start | bytes 1179648 | tf_op jit(solution)/shard_map/all_gather | solution.py:101
  7.9 155.1 %all-gather.6.cloned.1.call-start = ((), (), s32[]{:S(2)}) async-start(), calls=%async_computation | async-start | bytes 4718592 | tf_op jit(solution)/shard_map/all_gather | solution.py:91
  8.6 305.1 %all-gather.10.cloned.1.call-start = ((), (), s32[]{:S(2)}) async-start(), calls=%async_computation.2 | async-start | bytes 2129920 | tf_op jit(solution)/shard_map/all_gather | solution.py:116
  32.6 422.6 %all-gather.8.cloned.1.call-start = ((), (), s32[]{:S(2)}) async-start(), calls=%async_computation.1 | async-start | bytes 2129920 | tf_op jit(solution)/shard_map/all_gather | solution.py:117
  58.1 560.4 %all-gather.14.cloned.1.call-start = ((), (), s32[]{:S(2)}) async-start(), calls=%async_computation.4 | async-start | bytes 8519680 | tf_op jit(solution)/shard_map/all_gather | solution.py:115
  463.1 162.5 %copy-start = (bf16[16,32,256]{2,1,0:T(8,128)(2,1)}, bf16[16,32,256]{2,1,0:T(8,128)(2,1)S(1)}, u32[]{:S(2)}) copy-start(bf16[16,32,256]{2,1,0:T(8,128)(2,1)S(1)} %scatter_fusion) | copy-start | bytes 786436
Sparse Core Ops, SparseCore 0:
  10.1 49.9 all-gather.11
  62.2 100.7 all-gather.5
  166.8 146.8 all-gather.9
  316.9 138.1 all-gather.7
  458.9 159.5 all-gather.13
where the time goes:
time: 635 us
  waiting for transfers between devices  538 us (85%)
  blocking collectives  48.1 us (8%)
  matrix products  17 us (3%)
  between operations  13.9 us (2%)
  other arithmetic  10.5 us (2%)
  local copies, waits for them, and re-layouts  7.36 us (1%)
    all_gather x1, waiting for transfers between devices, on_device(): lax.all_gather(local_query, 'dp', axis=0, tiled=True)  155 us
    all_gather x1, waiting for transfers between devices, on_device(): lax.all_gather(local_key, 'dp', axis=0, tiled=True)  148 us
    all_gather x1, waiting for transfers between devices, on_device(): lax.all_gather(local_value, 'dp', axis=0, tiled=True)  136 us
    all_gather x1, waiting for transfers between devices, on_device(): tokens = lax.all_gather(hidden, 'tensor', axis=1, tiled=True)  94.6 us
    all_gather x1, blocking collectives, on_device(): lax.all_gather(value_weight, 'tensor', axis=0, tiled=True)  24.8 us
    all_gather x1, blocking collectives, on_device(): lax.all_gather(key_weight, 'tensor', axis=0, tiled=True)  23.3 us
    dot_general x3, matrix products, add_rows(): return jnp.dot(normed, shard_rows, preferred_element_type=jnp.float32)  16.3 us
  transfers between devices with their start and end apart: 5, of which 5 were waited for; matrix products, arithmetic and copies ran while one was open for 4% of the time, Pallas kernels for 0%

commit v1 on v0

--- a/solution.py
+++ b/solution.py
@@ -113,7 +113,9 @@
 
     shard_rows = (
         lax.all_gather(local_query, "dp", axis=0, tiled=True),
-        lax.all_gather(local_key, "dp", axis=0, tiled=True),
+        jnp.concatenate(
+            lax.all_to_all(jnp.stack([local_key] * lax.axis_size("dp")), "dp", 0, 0), axis=0
+        ),
         lax.all_gather(local_value, "dp", axis=0, tiled=True),
     )
     proj_query = add_rows(shard_rows[0])

time: 635 us -> 511 us (0.80)
  waiting for transfers between devices: 538 us -> 391 us
  starting transfers between devices: 0.2 us -> 29.5 us
    all_gather x1 -> x0, waiting for transfers between devices: 148 us -> none  [on_device(): lax.all_gather(local_key, 'dp', axis=0, tiled=True)]
    all_gather x1, waiting for transfers between devices: 94.6 us -> 61.1 us  [on_device(): tokens = lax.all_gather(hidden, 'tensor', axis=1, tiled=True)]
    all_to_all x0 -> x1, starting transfers between devices: none -> 29.4 us  [on_device(): lax.all_to_all(jnp.stack([local_key] * lax.axis_size('dp')), 'dp', 0, 0)]
    all_gather x1, waiting for transfers between devices: 1.91 us -> 25.8 us  [on_device(): lax.all_gather(query_weight, 'tensor', axis=0, tiled=True)]
    all_gather x1, waiting for transfers between devices: 136 us -> 152 us  [on_device(): lax.all_gather(local_value, 'dp', axis=0, tiled=True)]
  transfers between devices with their start and end apart: 5 -> 5, of which waited for: 5 -> 4; matrix products, arithmetic and copies ran while one was open for 4% -> 4% of each run, Pallas kernels for 0% -> 0%
where the time goes in v1:
time: 511 us
  waiting for transfers between devices  391 us (77%)
  blocking collectives  46 us (9%)
  starting transfers between devices  29.5 us (6%)
  matrix products  16.4 us (3%)
  between operations  14.1 us (3%)
  local copies, waits for them, and re-layouts  8.61 us (2%)
  other arithmetic  5.15 us (1%)
    all_gather x1, waiting for transfers between devices, on_device(): lax.all_gather(local_value, 'dp', axis=0, tiled=True)  152 us
    all_gather x1, waiting for transfers between devices, on_device(): lax.all_gather(local_query, 'dp', axis=0, tiled=True)  151 us
    all_gather x1, waiting for transfers between devices, on_device(): tokens = lax.all_gather(hidden, 'tensor', axis=1, tiled=True)  61.1 us
    all_to_all x1, starting transfers between devices, on_device(): lax.all_to_all(jnp.stack([local_key] * lax.axis_size('dp')), 'dp', 0, 0)  29.4 us
    all_gather x1, waiting for transfers between devices, on_device(): lax.all_gather(query_weight, 'tensor', axis=0, tiled=True)  25.8 us
    all_gather x1, blocking collectives, on_device(): lax.all_gather(value_weight, 'tensor', axis=0, tiled=True)  23.3 us
    all_gather x1, blocking collectives, on_device(): lax.all_gather(key_weight, 'tensor', axis=0, tiled=True)  22.8 us
    dot_general x3, matrix products, add_rows(): return jnp.dot(normed, shard_rows, preferred_element_type=jnp.float32)  15.6 us
  transfers between devices with their start and end apart: 5, of which 4 were waited for; matrix products, arithmetic and copies ran while one was open for 4% of the time, Pallas kernels for 0%

profile of v1, /device:TPU:1, one launch (start us, length us, event | category | flops | bytes accessed | tf_op | source)
XLA Modules:
  0.0 511.2 jit_solution(8097800636988815179)
XLA Ops:
  7.3 0.7 all-gather.9.cloned.1.call-update
  8.0 0.7 all-gather.5.cloned.1.call-update
  8.8 23.3 %all_gather.19 = bf16[128,1024]{1,0:T(8,128)(2,1)S(1)} all-gather(bf16[16,1024]{1,0:T(8,128)(2,1)} %param.14), channel_id=1, replica_groups=mesh['dp'=64,'tensor'=8] {'tensor'}, dimensions={0}, use_global_device_ids=true | all-gather | bytes 294912 | tf_op jit(solution)/shard_map/all_gather | solution.py:103
  32.0 0.6 constant_dynamic-slice_fusion.2
  32.7 25.8 %all-gather.9.cloned.1.call-done = bf16[128,4096]{1,0:T(8,128)(2,1)} async-done(((bf16[16,4096]{1,0:T(8,128)(2,1)}), bf16[128,4096]{1,0:T(8,128)(2,1)}) %all-gather.9.cloned.1.call-update) | async-done | bytes 1048592 | tf_op jit(solution)/shard_map/all_gather | solution.py:101
  58.6 1.6 constant_dynamic-slice_fusion
  60.2 22.8 %all_gather.21 = bf16[128,1024]{1,0:T(8,128)(2,1)S(1)} all-gather(bf16[16,1024]{1,0:T(8,128)(2,1)} %param.13), channel_id=1, replica_groups=mesh['dp'=64,'tensor'=8] {'tensor'}, dimensions={0}, use_global_device_ids=true | all-gather | bytes 294912 | tf_op jit(solution)/shard_map/all_gather | solution.py:102
  82.9 1.8 stack.4
  84.8 29.4 %all-to-all-start = ((bf16[64,128,128]{2,1,0:T(8,128)(2,1)}), bf16[64,128,128]{2,1,0:T(8,128)(2,1)S(1)}, u32[]{:S(2)}, u32[]{:S(2)}) async-start(bf16[64,128,128]{2,1,0:T(8,128)(2,1)} %stack.4), calls=%async_computation | async-start | bytes 4194304 | tf_op jit(solution)/shard_map/all_to_all | solution.py:117
  115.0 0.5 multiply_cosine_fusion
  115.6 61.1 %all-gather.5.cloned.1.call-done = bf16[256,8192]{1,0:T(8,128)(2,1)} async-done(((bf16[256,1024]{1,0:T(8,128)(2,1)}), bf16[256,8192]{1,0:T(8,128)(2,1)}) %all-gather.5.cloned.1.call-update) | async-done | bytes 4194320 | tf_op jit(solution)/shard_map/all_gather | solution.py:91
  176.7 3.1 fusion
  179.8 152.2 %all-gather.7.cloned.1.call-done = bf16[8192,128]{1,0:T(8,128)(2,1)} async-done(((bf16[128,128]{1,0:T(8,128)(2,1)}), bf16[8192,128]{1,0:T(8,128)(2,1)}) %all-gather.7.cloned.1.call-update) | async-done | bytes 2097168 | tf_op jit(solution)/shard_map/all_gather | solution.py:119
  332.0 4.6 fusion.6
  336.6 3.9 fusion.5
  340.6 0.3 fusion.18
  341.0 2.0 gather_fusion
  343.2 1.0 scatter_fusion
  344.2 150.9 %all-gather.11.cloned.1.call-done = bf16[8192,512]{1,0:T(8,128)(2,1)} async-done(((bf16[128,512]{1,0:T(8,128)(2,1)}), bf16[8192,512]{1,0:T(8,128)(2,1)}) %all-gather.11.cloned.1.call-update) | async-done | bytes 8388624 | tf_op jit(solution)/shard_map/all_gather | solution.py:115
  495.1 7.0 %convolution_add_fusion = f32[256,512]{1,0:T(8,128)S(1)} fusion(bf16[8192,512]{1,0:T(8,128)(2,1)} %all-gather.11.cloned.1.call-done, f32[512]{0:T(512)S(1)} %convert_element_type.69, bf16[256,8192]{1,0:T(8,128)(2,1)} %all-gather.5.cloned.1.call-done, f32[8192]{0:T(1024)S(1)} %convert_element_type.62, f32[256]{0:T(256)S(1)} %add_rsqrt_fusion), kind=kOutput, calls=%fused_computation.10 | convolution fusion | flops 2156003328 | bytes 13143040 | tf_op jit(solution)/shard_map/dot_general | solution.py:112
  502.4 0.3 fusion.32
  502.8 0.4 fusion.33
  503.4 0.3 convolution_convert_fusion
  503.8 0.8 copy.29
  (48 shorter events, 1.8 us)
Async XLA Ops:
  7.2 107.0 %copy-start.1 = (bf16[8192]{0:T(1024)(128)(2,1)S(1)}, bf16[8192]{0:T(1024)(128)(2,1)}, u32[]{:S(2)}) copy-start(bf16[8192]{0:T(1024)(128)(2,1)} %param.11) | copy-start | bytes 49156
  7.2 107.0 %copy-start.2 = (bf16[512]{0:T(512)(128)(2,1)S(1)}, bf16[512]{0:T(512)(128)(2,1)}, u32[]{:S(2)}) copy-start(bf16[512]{0:T(512)(128)(2,1)} %param.15) | copy-start | bytes 3076
  7.2 107.0 %copy-start.3 = (s32[1,4]{1,0:T(1,128)S(1)}, s32[1,4]{1,0:T(1,128)}, u32[]{:S(2)}) copy-start(s32[1,4]{1,0:T(1,128)} %param.18) | copy-start | bytes 52
  7.2 107.2 %copy-start.4 = (bf16[128]{0:T(256)(128)(2,1)S(1)}, bf16[128]{0:T(256)(128)(2,1)}, u32[]{:S(2)}) copy-start(bf16[128]{0:T(256)(128)(2,1)} %param.16) | copy-start | bytes 772
  7.2 107.2 %copy-start.5 = (bf16[128]{0:T(256)(128)(2,1)S(1)}, bf16[128]{0:T(256)(128)(2,1)}, u32[]{:S(2)}) copy-start(bf16[128]{0:T(256)(128)(2,1)} %param.17) | copy-start | bytes 772
  7.2 107.6 %copy-start.6 = (s32[1,16]{1,0:T(1,128)S(1)}, s32[1,16]{1,0:T(1,128)}, u32[]{:S(2)}) copy-start(s32[1,16]{1,0:T(1,128)} %param.19) | copy-start | bytes 196
  7.2 51.3 %all-gather.9.cloned.1.call-start = ((), (), s32[]{:S(2)}) async-start(), calls=%async_computation.3 | async-start | bytes 1179648 | tf_op jit(solution)/shard_map/all_gather | solution.py:101
  8.0 168.7 %all-gather.5.cloned.1.call-start = ((), (), s32[]{:S(2)}) async-start(), calls=%async_computation.1 | async-start | bytes 4718592 | tf_op jit(solution)/shard_map/all_gather | solution.py:91
  8.7 323.3 %all-gather.7.cloned.1.call-start = ((), (), s32[]{:S(2)}) async-start(), calls=%async_computation.2 | async-start | bytes 2129920 | tf_op jit(solution)/shard_map/all_gather | solution.py:119
  32.7 462.4 %all-gather.11.cloned.1.call-start = ((), (), s32[]{:S(2)}) async-start(), calls=%async_computation.4 | async-start | bytes 8519680 | tf_op jit(solution)/shard_map/all_gather | solution.py:115
  84.8 251.8 %all-to-all-start = ((bf16[64,128,128]{2,1,0:T(8,128)(2,1)}), bf16[64,128,128]{2,1,0:T(8,128)(2,1)S(1)}, u32[]{:S(2)}, u32[]{:S(2)}) async-start(bf16[64,128,128]{2,1,0:T(8,128)(2,1)} %stack.4), calls=%async_computation | async-start | bytes 4194304 | tf_op jit(solution)/shard_map/all_to_all | solution.py:117
  344.2 158.0 %copy-start = (bf16[16,32,256]{2,1,0:T(8,128)(2,1)}, bf16[16,32,256]{2,1,0:T(8,128)(2,1)S(1)}, u32[]{:S(2)}) copy-start(bf16[16,32,256]{2,1,0:T(8,128)(2,1)S(1)} %scatter_fusion) | copy-start | bytes 786436
Sparse Core Ops, SparseCore 0:
  10.1 48.3 all-gather.8
  60.6 115.9 all-gather.4
  180.5 151.4 all-gather.6
  335.7 159.3 all-gather.10
